TPU v7x, 128 devices: a whole 4x4x4 slice. The times are simulated.
128 devices in a mesh: hst: 16 (over z, x_hi, core), head: 8 (over y, x_lo).
Axes of the slice: x: 4 (x_hi: 2, x_lo: 2; x = x_hi * 2 + x_lo), y: 4, z: 4, core: 2. Of those that a mesh axis runs over, the one named last changes fastest.
Arguments:
- query_rows: bfloat16 [16384, 8192], P(('hst', 'head')), may hold values from -9 to 9
- token_keys: bfloat16 [16384, 1024], P(('hst', 'head')), may hold values from -9 to 9
- token_values: bfloat16 [16384, 1024], P(('hst', 'head')), may hold values from -6 to 6
- offsets: int32 [16], P('hst'), may hold values from 0 to 4095
- anchor_owner: int32 [1], replicated, may hold values from 0 to 15
Outputs:
- attended: bfloat16 [16384, 8192], P(('hst', 'head'))
Inputs may be any that keep to these rules, and one draw needn't show every extreme that they name: `offsets`: positions of block starts. `anchor_owner`: index of a block.
All inputs are finite; a program needn't handle non-finite values.
Results may differ from a plain program's by a relative error of at most 0.0095.
The roundings to bfloat16 on the way count: a program that leaves them out, or rounds other values in their place, can miss the bound.
Values may be sent and summed in bfloat16 or wider, within the bound.
A program may use at most 64 MiB of HBM per device.

v0:
```python
import jax
import jax.numpy as jnp
from jax import lax
from jax.sharding import PartitionSpec as P

QUERY_HEADS = 64
KEY_VALUE_HEADS = 8
HEAD_SIZE = 128


rope_theta = 500000.0


def spread(value, axis, root):
    mine = lax.axis_index(axis) == root
    return lax.psum(jnp.where(mine, value, jnp.zeros_like(value)), axis)


def apply_rotary(value_matrix, token_positions):
    width = value_matrix.shape[-1]
    half = width // 2
    exponents = jnp.arange(half, dtype=jnp.float32) * (2.0 / width)
    inverse = jnp.float32(rope_theta) ** (-exponents)
    angles = token_positions.astype(jnp.float32)[:, None] * inverse[None, :]
    doubled = jnp.concatenate([angles, angles], 1)
    cosine = jnp.cos(doubled)[:, None, :]
    sine = jnp.sin(doubled)[:, None, :]
    floats = value_matrix.astype(jnp.float32)
    turned = jnp.concatenate([-floats[..., half:], floats[..., :half]], -1)
    return (floats * cosine + turned * sine).astype(jnp.bfloat16)


def attend(queries, keys_local, values_local, keys_anchor, values_anchor, query_index, with_anchor):
    count = keys_local.shape[0]
    keys_all = jnp.concatenate([keys_anchor, keys_local], 0)
    values_all = jnp.concatenate([values_anchor, values_local], 0)
    scale = queries.shape[-1] ** (-0.5)
    scores = (
        jnp.einsum("rgd,kd->grk", queries, keys_all, preferred_element_type=jnp.float32) * scale
    )
    column = jnp.arange(2 * count, dtype=jnp.int32)
    allowed = jnp.where(
        column[None, :] < count, with_anchor, column[None, :] - count <= query_index[:, None]
    )
    peak = jnp.max(jnp.where(allowed[None], scores, -jnp.inf), -1, keepdims=True)
    weights = jnp.where(allowed[None], jnp.exp(scores - peak), jnp.float32(0.0))
    total = jnp.sum(weights, -1, keepdims=True)
    mixed = (
        jnp.einsum(
            "grk,kd->grd",
            weights.astype(jnp.bfloat16),
            values_all,
            preferred_element_type=jnp.float32,
        )
        / total
    )
    return jnp.transpose(mixed, (1, 0, 2)).astype(jnp.bfloat16)


def local(query_rows, token_keys, token_values, offsets, anchor_owner):
    query_group = QUERY_HEADS // KEY_VALUE_HEADS
    nearby_rows = query_rows.shape[0]
    chosen = anchor_owner[0]
    with_anchor = lax.axis_index("hst") != chosen
    first_row = lax.axis_index("head") * nearby_rows
    query_index = first_row + jnp.arange(nearby_rows, dtype=jnp.int32)
    token_positions = offsets[0] + query_index
    spun_keys = apply_rotary(
        token_keys.reshape(nearby_rows, KEY_VALUE_HEADS, HEAD_SIZE), token_positions
    )
    unrotated_values = token_values.reshape(nearby_rows, KEY_VALUE_HEADS, HEAD_SIZE)
    spun_queries = apply_rotary(
        query_rows.reshape(nearby_rows, QUERY_HEADS, HEAD_SIZE), token_positions
    ).reshape(nearby_rows, KEY_VALUE_HEADS, query_group, HEAD_SIZE)
    anchor_k, anchor_v = (spread(spun_keys, "hst", chosen), spread(unrotated_values, "hst", chosen))
    block_k, block_v, block_ak, block_av = (
        lax.all_gather(spun_keys, "head", axis=0, tiled=True),
        lax.all_gather(unrotated_values, "head", axis=0, tiled=True),
        lax.all_gather(anchor_k, "head", axis=0, tiled=True),
        lax.all_gather(anchor_v, "head", axis=0, tiled=True),
    )

    def per_kv_head(pieces):
        group_q, own_k, own_v, far_k, far_v = pieces
        return attend(group_q, own_k, own_v, far_k, far_v, query_index, with_anchor)

    mixed = lax.map(
        per_kv_head,
        (
            jnp.transpose(spun_queries, (1, 0, 2, 3)),
            jnp.transpose(block_k, (1, 0, 2)),
            jnp.transpose(block_v, (1, 0, 2)),
            jnp.transpose(block_ak, (1, 0, 2)),
            jnp.transpose(block_av, (1, 0, 2)),
        ),
    )
    return jnp.transpose(mixed, (1, 0, 2, 3)).reshape(nearby_rows, QUERY_HEADS * HEAD_SIZE)


def solution(mesh):
    return jax.shard_map(
        local,
        mesh=mesh,
        in_specs=(
            P(("hst", "head"), None),
            P(("hst", "head"), None),
            P(("hst", "head"), None),
            P("hst"),
            P(),
        ),
        out_specs=P(("hst", "head"), None),
        check_vma=False,
    )
```

profile of v0, /device:TPU:27, one launch (start us, length us, event | category | flops | bytes accessed | tf_op | source)
XLA Modules:
  0.0 411.5 jit_solution(11083561010181679160)
XLA Ops:
  13.5 166.2 %all-reduce.3.cloned.1.call-done = (bf16[128,8,128]{0,2,1:T(8,128)(2,1)}, bf16[128,8,128]{0,2,1:T(8,128)(2,1)}) async-done(((bf16[128,8,128]{0,2,1:T(8,128)(2,1)}, bf16[128,8,128]{0,2,1:T(8,128)(2,1)}), (bf16[128,8,128]{0,2,1:T(8,128)(2,1)}, bf16[128,8,128]{0,2,1:T(8,128)(2,1)})) %all-reduce.3.cloned.1.call-update) | async-done | bytes 524304 | tf_op jit(solution)/shard_map/psum | solution.py:16
  180.4 3.2 copy.12
  185.9 3.1 slice_negate_fusion
  189.3 2.4 fusion.53
  191.7 38.9 %all-gather.9.cloned.1.call-done = bf16[1024,8,128]{0,2,1:T(8,128)(2,1)} async-done(((bf16[128,8,128]{0,2,1:T(8,128)(2,1)}), bf16[1024,8,128]{0,2,1:T(8,128)(2,1)}) %all-gather.9.cloned.1.call-update) | async-done | bytes 2097168 | tf_op jit(solution)/shard_map/all_gather | solution.py:80
  230.6 53.8 %all-gather.5.cloned.1.call-done = bf16[1024,8,128]{0,2,1:T(8,128)(2,1)} async-done(((bf16[128,8,128]{0,2,1:T(8,128)(2,1)}), bf16[1024,8,128]{0,2,1:T(8,128)(2,1)}) %all-gather.5.cloned.1.call-update) | async-done | bytes 2097168 | tf_op jit(solution)/shard_map/all_gather | solution.py:79
  284.4 115.0 %while.13 = (s32[]{:T(128)}, bf16[8,128,8,128]{3,1,2,0:T(8,128)(2,1)S(1)}, pred[]{:T(512)}, bf16[8,1024,128]{1,2,0:T(8,128)(2,1)}, bf16[8,1024,128]{1,2,0:T(8,12...) while((s32[]{:T(128)}, ...), condition=%wide.region_5.6_spmd.clone, body=%wide.region_2.5_spmd.clone.sunk | while | flops 1629231232 | bytes 15759478 | solution.py:87
  287.3 6.4 %fusion.73 = (f32[8,128]{1,0:T(8,128)S(1)}, bf16[8,128,2048]{1,2,0:T(8,128)(2,1)}) fusion(pred[128,2048]{0,1:T(8,128)(4,1)S(1)} %compare_select_fusion.2, bf16[1024,128]{1,0:T(8,128)(2,1)S(1)} %bitcast.118, bf16[1024,128]{1,0:T(8,128)(2,1)S(1)} %bitcast.119, bf16[8,128,8,128]{1,3,2,0:T(8,128)(2,1)} %get-tuple-element.275, s32[]{:T(128)} %get-tuple-element.260), kind=kOutput, calls=%fused_computation.61.clone.1 | convolution fusion | flops 1090521088 | bytes 6296576 | tf_op jit(solution)/shard_map/while/body/eval_jaxpr/sub | solution.py:46
  295.1 3.6 fusion.74
  301.7 6.4 %fusion.73 = (f32[8,128]{1,0:T(8,128)S(1)}, bf16[8,128,2048]{1,2,0:T(8,128)(2,1)}) fusion(pred[128,2048]{0,1:T(8,128)(4,1)S(1)} %compare_select_fusion.2, bf16[1024,128]{1,0:T(8,128)(2,1)S(1)} %bitcast.118, bf16[1024,128]{1,0:T(8,128)(2,1)S(1)} %bitcast.119, bf16[8,128,8,128]{1,3,2,0:T(8,128)(2,1)} %get-tuple-element.275, s32[]{:T(128)} %get-tuple-element.260), kind=kOutput, calls=%fused_computation.61.clone.1 | convolution fusion | flops 1090521088 | bytes 6296576 | tf_op jit(solution)/shard_map/while/body/eval_jaxpr/sub | solution.py:46
  309.5 3.6 fusion.74
  316.1 6.4 %fusion.73 = (f32[8,128]{1,0:T(8,128)S(1)}, bf16[8,128,2048]{1,2,0:T(8,128)(2,1)}) fusion(pred[128,2048]{0,1:T(8,128)(4,1)S(1)} %compare_select_fusion.2, bf16[1024,128]{1,0:T(8,128)(2,1)S(1)} %bitcast.118, bf16[1024,128]{1,0:T(8,128)(2,1)S(1)} %bitcast.119, bf16[8,128,8,128]{1,3,2,0:T(8,128)(2,1)} %get-tuple-element.275, s32[]{:T(128)} %get-tuple-element.260), kind=kOutput, calls=%fused_computation.61.clone.1 | convolution fusion | flops 1090521088 | bytes 6296576 | tf_op jit(solution)/shard_map/while/body/eval_jaxpr/sub | solution.py:46
  323.9 3.6 fusion.74
  330.5 6.4 %fusion.73 = (f32[8,128]{1,0:T(8,128)S(1)}, bf16[8,128,2048]{1,2,0:T(8,128)(2,1)}) fusion(pred[128,2048]{0,1:T(8,128)(4,1)S(1)} %compare_select_fusion.2, bf16[1024,128]{1,0:T(8,128)(2,1)S(1)} %bitcast.118, bf16[1024,128]{1,0:T(8,128)(2,1)S(1)} %bitcast.119, bf16[8,128,8,128]{1,3,2,0:T(8,128)(2,1)} %get-tuple-element.275, s32[]{:T(128)} %get-tuple-element.260), kind=kOutput, calls=%fused_computation.61.clone.1 | convolution fusion | flops 1090521088 | bytes 6296576 | tf_op jit(solution)/shard_map/while/body/eval_jaxpr/sub | solution.py:46
  338.3 3.6 fusion.74
  344.9 6.4 %fusion.73 = (f32[8,128]{1,0:T(8,128)S(1)}, bf16[8,128,2048]{1,2,0:T(8,128)(2,1)}) fusion(pred[128,2048]{0,1:T(8,128)(4,1)S(1)} %compare_select_fusion.2, bf16[1024,128]{1,0:T(8,128)(2,1)S(1)} %bitcast.118, bf16[1024,128]{1,0:T(8,128)(2,1)S(1)} %bitcast.119, bf16[8,128,8,128]{1,3,2,0:T(8,128)(2,1)} %get-tuple-element.275, s32[]{:T(128)} %get-tuple-element.260), kind=kOutput, calls=%fused_computation.61.clone.1 | convolution fusion | flops 1090521088 | bytes 6296576 | tf_op jit(solution)/shard_map/while/body/eval_jaxpr/sub | solution.py:46
  352.7 3.6 fusion.74
  359.2 6.4 %fusion.73 = (f32[8,128]{1,0:T(8,128)S(1)}, bf16[8,128,2048]{1,2,0:T(8,128)(2,1)}) fusion(pred[128,2048]{0,1:T(8,128)(4,1)S(1)} %compare_select_fusion.2, bf16[1024,128]{1,0:T(8,128)(2,1)S(1)} %bitcast.118, bf16[1024,128]{1,0:T(8,128)(2,1)S(1)} %bitcast.119, bf16[8,128,8,128]{1,3,2,0:T(8,128)(2,1)} %get-tuple-element.275, s32[]{:T(128)} %get-tuple-element.260), kind=kOutput, calls=%fused_computation.61.clone.1 | convolution fusion | flops 1090521088 | bytes 6296576 | tf_op jit(solution)/shard_map/while/body/eval_jaxpr/sub | solution.py:46
  367.1 3.6 fusion.74
  373.6 6.4 %fusion.73 = (f32[8,128]{1,0:T(8,128)S(1)}, bf16[8,128,2048]{1,2,0:T(8,128)(2,1)}) fusion(pred[128,2048]{0,1:T(8,128)(4,1)S(1)} %compare_select_fusion.2, bf16[1024,128]{1,0:T(8,128)(2,1)S(1)} %bitcast.118, bf16[1024,128]{1,0:T(8,128)(2,1)S(1)} %bitcast.119, bf16[8,128,8,128]{1,3,2,0:T(8,128)(2,1)} %get-tuple-element.275, s32[]{:T(128)} %get-tuple-element.260), kind=kOutput, calls=%fused_computation.61.clone.1 | convolution fusion | flops 1090521088 | bytes 6296576 | tf_op jit(solution)/shard_map/while/body/eval_jaxpr/sub | solution.py:46
  381.4 3.6 fusion.74
  388.0 6.4 %fusion.73 = (f32[8,128]{1,0:T(8,128)S(1)}, bf16[8,128,2048]{1,2,0:T(8,128)(2,1)}) fusion(pred[128,2048]{0,1:T(8,128)(4,1)S(1)} %compare_select_fusion.2, bf16[1024,128]{1,0:T(8,128)(2,1)S(1)} %bitcast.118, bf16[1024,128]{1,0:T(8,128)(2,1)S(1)} %bitcast.119, bf16[8,128,8,128]{1,3,2,0:T(8,128)(2,1)} %get-tuple-element.275, s32[]{:T(128)} %get-tuple-element.260), kind=kOutput, calls=%fused_computation.61.clone.1 | convolution fusion | flops 1090521088 | bytes 6296576 | tf_op jit(solution)/shard_map/while/body/eval_jaxpr/sub | solution.py:46
  395.8 3.6 fusion.74
  400.8 3.1 copy.28
  (114 shorter events, 43.9 us)
Async XLA Ops:
  7.4 2.9 copy-start.3
  7.4 172.3 %all-reduce.3.cloned.1.call-start = ((), (), s32[]{:S(2)}) async-start(), calls=%async_computation.4 | async-start | bytes 1048576 | tf_op jit(solution)/shard_map/psum | solution.py:16
  10.5 2.4 copy-start.1
  12.2 179.5 %all-gather.7.cloned.1.call-start = ((), (), s32[]{:S(2)}) async-start(), calls=%async_computation.1 | async-start | bytes 2359296 | tf_op jit(solution)/shard_map/all_gather | solution.py:77
  12.8 178.9 %all-gather.11.cloned.1.call-start = ((), (), s32[]{:S(2)}) async-start(), calls=%async_computation.3 | async-start | bytes 2359296 | tf_op jit(solution)/shard_map/all_gather | solution.py:78
  13.4 217.2 %all-gather.9.cloned.1.call-start = ((), (), s32[]{:S(2)}) async-start(), calls=%async_computation.2 | async-start | bytes 2359296 | tf_op jit(solution)/shard_map/all_gather | solution.py:80
  179.7 104.7 %all-gather.5.cloned.1.call-start = ((), (), s32[]{:S(2)}) async-start(), calls=%async_computation | async-start | bytes 2359296 | tf_op jit(solution)/shard_map/all_gather | solution.py:79
  185.9 3.5 copy-start
  189.3 95.0 %copy-start.2 = (bf16[8,128,8,128]{3,1,2,0:T(8,128)(2,1)S(1)}, bf16[8,128,8,128]{3,1,2,0:T(8,128)(2,1)}, u32[]{:S(2)}) copy-start(bf16[8,128,8,128]{3,1,2,0:T(8,128)(2,1)} %custom-call) | copy-start | bytes 6291460
Sparse Core Ops, SparseCore 0:
  12.4 167.2 all-reduce.2
Sparse Core Ops, SparseCore 1:
  14.3 52.9 all-gather.6
  68.7 52.2 all-gather.10
  179.8 50.8 all-gather.8
  232.3 52.0 all-gather.4
where the time goes:
time: 415 us; the launch traced here: 412 us
  waiting for transfers between devices  261 us (63%)
  matrix products  79.8 us (19%)
  local copies, waits for them, and re-layouts  31.9 us (8%)
  other arithmetic  21.9 us (5%)
  between operations  16.5 us (4%)
    psum x1, waiting for transfers between devices, spread(): return lax.psum(jnp.where(mine, value, jnp.zeros_like(value)), axis)  166 us
    all_gather x1, waiting for transfers between devices, local(): lax.all_gather(anchor_k, 'head', axis=0, tiled=True)  53.8 us
    sub x8, matrix products, attend(): weights = jnp.where(allowed[None], jnp.exp(scores - peak), jnp.float32(0.0))  51.2 us
    all_gather x1, waiting for transfers between devices, local(): lax.all_gather(anchor_v, 'head', axis=0, tiled=True)  38.9 us
    dot_general x8, matrix products, attend(): jnp.einsum('grk,kd->grd', weights.astype(jnp.bfloat16), values_all, prefe...  28.6 us
    dynamic_slice x48, local copies, waits for them, and re-layouts, local(): lax.map(per_kv_head, (jnp.transpose(spun_queries, (1, 0, 2, 3)), jnp.tran...  22.5 us
    select_n x8, other arithmetic, attend(): jnp.where(column[None, :] < count, with_anchor, column[None, :] - count <...  12 us
  transfers between devices with their start and end apart: 5, of which 3 were waited for; matrix products, arithmetic and copies ran while one was open for 3% of the time, Pallas kernels for 0%

commit v1 on v0

v1 whole, which is shorter than its diff:
```python
import functools

import jax
import jax.numpy as jnp
import numpy as np
from jax import lax
from jax.experimental import pallas as pl
from jax.experimental.pallas import tpu as pltpu
from jax.sharding import PartitionSpec as P

QUERY_HEADS = 64
KV = 8
D = 128
TOK = 128
ROPE_THETA = 500000.0
LOG2E_SCALE = float(D**-0.5 * np.log2(np.e))
F32 = jnp.float32
BF16 = jnp.bfloat16
MESH = pl.DeviceIdType.MESH
NT = (((1,), (1,)), ((), ()))
R = 512
MASKED = -1e30


def kernel(
    q_ref, k_ref, v_ref, inv_ref, off_ref, own_ref, out_ref,
    q_in, out_scr, kvl, kva, cand2, chosen, cand8, qs, s_scr, m_scr, bias, onesl, cos_scr, sin_scr,
    q_sem, out_sem, k1s, k1r, v1s, v1r, k2s, k2r, v3s, v3r, k3s,
    ps, pr, a0s, a0r, a2s, a2r, a3s, a3r, cxs, cxr,
):
    hst = lax.axis_index("hst")
    head = lax.axis_index("head")
    z, xh, c = hst // 4, (hst // 2) % 2, hst % 2
    y, xl = head // 2, head % 2
    h0 = 2 * z + xh

    def wrap(i, n):
        return jnp.where(i >= n, i - n, i)

    def dev(zz, xxh, cc, yy, xxl):
        return ((zz * 2 + xxh) * 2 + cc, yy * 2 + xxl)

    partner = dev(z, xh, c, y, 1 - xl)
    other = dev(z, xh, 1 - c, y, xl)
    zs = [z] + [wrap(z + d, 4) for d in (1, 2, 3)]
    ys = [y] + [wrap(y + d, 4) for d in (1, 2, 3)]

    def flipped(bit, flip):
        return 1 - bit if flip else bit

    def along(dz, flip):
        return dev(zs[dz], flipped(xh, flip), c, y, flipped(xl, flip))

    def beside(dy, flip):
        return dev(z, xh, c, ys[dy], flipped(xl, flip))

    CHIPS = [(0, 1), (1, 0), (3, 0), (1, 1), (3, 1), (2, 0), (2, 1)]
    BLOCK = [(0, 1), (1, 0), (1, 1), (3, 0), (3, 1), (2, 0), (2, 1)]

    q_load = pltpu.make_async_copy(q_ref, q_in, q_sem)
    q_load.start()

    def store(h):
        cols = pl.ds(pl.multiple_of(h * 1024, 1024), 1024)
        return pltpu.make_async_copy(out_scr.at[:, cols], out_ref.at[:, cols], out_sem.at[h])

    bar = pltpu.get_barrier_semaphore()
    for device in [other] + [along(*e) for e in CHIPS] + [beside(*e) for e in BLOCK]:
        pl.semaphore_signal(bar, inc=1, device_id=device, device_id_type=MESH)

    start = (off_ref[0] + head * TOK).astype(F32)
    pos = lax.broadcasted_iota(jnp.int32, (TOK, D), 0).astype(F32) + start
    lane = lax.broadcasted_iota(jnp.int32, (TOK, D), 1)
    ang = pos * inv_ref[...]
    cos_scr[...] = jnp.cos(ang)
    sine = jnp.sin(ang)
    sin_scr[...] = jnp.where(lane < D // 2, -sine, sine)

    def rotate(x):
        x = x.astype(F32)
        return (x * cos_scr[...] + pltpu.roll(x, D // 2, 1) * sin_scr[...]).astype(BF16)

    for h in range(KV):
        kvl[0, h, 3, xl] = rotate(k_ref[:, h * D:(h + 1) * D])
        kvl[1, h, 3, xl] = v_ref[:, h * D:(h + 1) * D]

    def rc(src, dst, ssem, rsem, device):
        return pltpu.make_async_remote_copy(
            src_ref=src, dst_ref=dst, send_sem=ssem, recv_sem=rsem, device_id=device, device_id_type=MESH
        )

    ZOFF = [0, 1, 3, 2]

    def two(g):
        return pl.ds(2 * zs[ZOFF[g]], 2)

    def c_k1(g):
        ref = kvl.at[:, two(g), 3, xl]
        return rc(ref, ref, k1s.at[g], k1r.at[g], partner)

    def c_v1(g, d):
        return rc(kvl.at[1, two(g), 3, xl], kvl.at[1, two(g), 3 - d, xl], v1s.at[g, d], v1r.at[g, d], beside(d, 0))

    def c_k2(g, d):
        return rc(kvl.at[0, two(g), 3], kvl.at[0, two(g), 3 - d], k2s.at[g, d], k2r.at[g, d], beside(d, 0))

    def c_v3(g, n):
        ref = kvl.at[1, two(g), pl.ds(3 - n, n), xl]
        return rc(ref, ref, v3s.at[g], v3r.at[g], partner)

    def c_k3(g, n):
        return rc(kvl.at[0, two(g), 0 if n == 3 else 2], kvl.at[0, two(g), 1], k3s.at[g], k2r.at[g, 2],
                  beside(3 if n == 3 else 1, 0))

    def ups(f, direct):
        for d, cond in ((3, y == 0), (1, y <= 2), (2, y <= 1)):
            if d != 2 or direct:
                @pl.when(cond)
                def _():
                    f(d)

    def at_y(f, ns=(1, 2, 3)):
        for n in ns:
            @pl.when(y == n)
            def _():
                f(n)

    def l1(g):
        c_k1(g).start()
        ups(lambda d: c_v1(g, d).start(), True)

    def l2k(g):
        c_k1(g).wait_recv()
        ups(lambda d: c_k2(g, d).start(), False)

    def l2v(g):
        for d in (1, 2, 3):
            @pl.when(y >= d)
            def _():
                c_v1(g, d).wait_recv()

        at_y(lambda n: c_v3(g, n).start())

    def l2c(g):
        def on(n):
            c_k2(g, 3 if n == 3 else 1).wait_recv()
            c_k3(g, n).start()

        at_y(on, (2, 3))

    def l3(g):
        @pl.when((y == 1) | (y == 3))
        def _():
            c_k2(g, 1).wait_recv()

        @pl.when(y >= 2)
        def _():
            c_k2(g, 2).wait_recv()

        at_y(lambda n: c_v3(g, n).wait_recv())

    def l_sent(g):
        c_k1(g).wait_send()
        ups(lambda d: c_v1(g, d).wait_send(), True)
        ups(lambda d: c_k2(g, d).wait_send(), False)
        at_y(lambda n: c_v3(g, n).wait_send())
        at_y(lambda n: c_k3(g, n).wait_send(), (2, 3))

    def c_p():
        return rc(kvl.at[1 - c, :, 3, xl], cand2.at[c], ps, pr, other)

    def c_p_in():
        return rc(cand2.at[1 - c], cand2.at[1 - c], ps, pr, other)

    def chip_head(e):
        return 2 * zs[e[0]] + flipped(xh, e[1])

    def c_a0(r):
        return rc(chosen.at[chip_head(CHIPS[r])], cand8.at[h0], a0s.at[r], a0r.at[h0], along(*CHIPS[r]))

    def c_a0_in(r):
        h = chip_head(CHIPS[r])
        return rc(cand8.at[h], cand8.at[h], a0s.at[r], a0r.at[h], along(*CHIPS[r]))

    def c_a2(r):
        ref = kva.at[c, h0, head]
        return rc(ref, ref, a2s.at[r], a2r.at[head], beside(*BLOCK[r]))

    def c_a2_in(r):
        s = 2 * ys[BLOCK[r][0]] + flipped(xl, BLOCK[r][1])
        ref = kva.at[c, h0, s]
        return rc(ref, ref, a2s.at[r], a2r.at[s], beside(*BLOCK[r]))

    def head_of(n):
        return h0 if n == 0 else chip_head(CHIPS[n - 1])

    def c_cx(n, kind):
        ref = kva.at[kind, head_of(n)]
        return rc(ref, ref, cxs.at[n], cxr.at[n], other)

    def to(n):
        dz, flip = CHIPS[n - 1]
        return along((4 - dz) % 4, flip)

    def c_a3(n):
        ref = kva.at[c, h0]
        return rc(ref, ref, a3s.at[n], a3r.at[n], to(n))

    def c_a3_on(n, keys):
        if keys:
            ref = kva.at[c, head_of(1)]
            return rc(ref, ref, a3s.at[n], a3r.at[n], along((4 - CHIPS[n - 1][0]) % 4, 0))
        ref = kva.at[c, head_of({4: 2, 5: 3, 7: 6}[n])]
        return rc(ref, ref, a3s.at[n], a3r.at[n], along(0, 1))

    def c_a3_in(n):
        ref = kva.at[c, head_of(n)]
        return rc(ref, ref, a3s.at[n], a3r.at[n], along(*CHIPS[n - 1]))

    def a_on(kind, *ns):
        @pl.when(c == kind)
        def _():
            for n in ns:
                c_a3_on(n, kind == 0).start()

    def a_in(n):
        c_a3_in(n).wait_recv()
        c_cx(n, c).start()
        if n == 1:
            a_on(0, 4, 5, 7)
        elif n in (2, 3, 6):
            a_on(1, {2: 4, 3: 5, 6: 7}[n])

    def cx_in(n):
        c_cx(n, 1 - c).wait_recv()

    penalty = jnp.where(own_ref[0] == hst, -MASKED, 0.0).astype(F32)

    def keys(src, h, t):
        if src is kva:
            return kva[0, h, 2 * t:2 * t + 2].reshape(256, D)
        return kvl[0, h, t].reshape(256, D)

    def qk(h, half, b):
        q = qs[pl.ds(pl.multiple_of((h * 8 + half * 4) * TOK, R), R), :]
        mx = []
        for part, src in ((0, kva), (1, kvl)):
            m = None
            for t in range(4):
                s = lax.dot_general(q, keys(src, h, t), NT, preferred_element_type=F32)
                if part == 1 and t == 3:
                    s = (s.reshape(R // TOK, TOK, 256) + bias[...][None]).reshape(R, 256)
                lo = part * 1024 + t * 256
                s_scr[b, :, lo:lo + 256] = s
                for u in range(2):
                    w = s[:, u * 128:(u + 1) * 128]
                    m = w if m is None else jnp.maximum(m, w)
            mx.append(m)
        m = jnp.maximum(mx[0] - penalty, mx[1])
        m_scr[b] = jnp.broadcast_to(jnp.max(m, 1, keepdims=True), (R, D)) * LOG2E_SCALE

    def pv(h, half, b):
        os = []
        for part, src in ((0, kva), (1, kvl)):
            m = m_scr[b] + penalty if part == 0 else m_scr[b]
            p = jnp.concatenate(
                [jnp.exp2(s_scr[b, :, lo:lo + 128] * LOG2E_SCALE - m).astype(BF16)
                 for lo in range(part * 1024, part * 1024 + 1024, 128)], 1)
            ones = jnp.ones((1024, D), BF16) if part == 0 else onesl[...]
            w = jnp.concatenate([src[1, h].reshape(1024, D), ones], 1)
            os.append(jnp.dot(p, w, preferred_element_type=F32))
        o = os[0] + os[1]
        o = (o[:, :D] / o[:, D:]).astype(BF16)
        for i in range(R // TOK):
            col = pl.multiple_of((h * 8 + half * 4 + i) * D, D)
            out_scr[:, pl.ds(col, D)] = o[i * TOK:(i + 1) * TOK]

    def rotate_queries(h, _):
        for i in range(8):
            col = pl.multiple_of((h * 8 + i) * D, D)
            qs[pl.ds(col, TOK), :] = rotate(q_in[:, pl.ds(col, D)])
        return 0

    pl.semaphore_wait(bar, 15)
    c_p().start()
    l1(0)
    l1(1)

    t_i = lax.broadcasted_iota(jnp.int32, (TOK, 256), 0)
    k_i = lax.broadcasted_iota(jnp.int32, (TOK, 256), 1)
    bias[...] = jnp.where(k_i <= t_i + xl * TOK, 0.0, MASKED).astype(F32)
    onesl[768:1024] = jnp.ones((256, D), BF16)
    cand2[c] = kvl[c, :, 3, xl]
    for d in (1, 2, 3):
        rows = slice((3 - d) * 256, (4 - d) * 256)

        @pl.when(y >= d)
        def _():
            onesl[rows] = jnp.ones((256, D), BF16)

        @pl.when(y < d)
        def _():
            onesl[rows] = jnp.zeros((256, D), BF16)

            def fill(h, _):
                first = kvl[0, h, 3, xl][0:1].astype(F32)
                kvl[0, h, 3 - d] = jnp.broadcast_to(first[None], (2, TOK, D)).astype(BF16)
                kvl[1, h, 3 - d] = jnp.zeros((2, TOK, D), BF16)
                return 0

            lax.fori_loop(0, KV, fill, 0)

    c_p_in().wait_recv()
    chosen[...] = cand2[own_ref[0] % 2]
    for r in range(7):
        c_a0(r).start()
    cand8[h0] = chosen[h0]
    q_load.wait()
    lax.fori_loop(0, 4, rotate_queries, 0)
    l2k(0)
    l2v(0)
    for r in range(7):
        c_a0_in(r).wait_recv()
    kva[c, h0, head] = cand8[own_ref[0] // 2]
    for r in range(7):
        c_a2(r).start()
    lax.fori_loop(4, 8, rotate_queries, 0)
    l2c(0)
    for r in range(7):
        c_a2_in(r).wait_recv()
    c_cx(0, c).start()
    for n in (1, 2, 3, 6):
        c_a3(n).start()
    l2k(1)
    l2v(1)
    l1(2)
    l1(3)
    l3(0)
    cx_in(0)

    qk(head_of(0), 0, 0)

    POLLS = {
        (0, 0): lambda: l2c(1),
        (0, 1): lambda: (l2k(2), l2v(2), a_in(1), a_in(2), a_in(3), cx_in(1)),
        (0, 2): lambda: (l2k(3), l2c(2), l3(1)),
        (0, 3): lambda: (l2v(3), cx_in(2)),
        (1, 0): lambda: l2c(3),
        (1, 1): lambda: (l3(2), cx_in(3)),
        (1, 2): lambda: (a_in(4), a_in(5), a_in(6)),
        (1, 3): lambda: cx_in(4),
        (2, 1): lambda: (cx_in(5), a_in(7)),
        (2, 2): lambda: l3(3),
        (2, 3): lambda: cx_in(6),
        (3, 1): lambda: cx_in(7),
    }

    def two_heads(it, _):
        def poll(j):
            for (i, jj), f in POLLS.items():
                if jj == j:
                    @pl.when(it == i)
                    def _():
                        f()

        def by_it(values):
            out = values[3]
            for i in (2, 1, 0):
                out = jnp.where(it == i, values[i], out)
            return out

        ha = by_it([head_of(n) for n in (0, 2, 4, 6)])
        hb = by_it([head_of(n) for n in (1, 3, 5, 7)])
        hn = by_it([head_of(n) for n in (2, 4, 6, 7)])

        poll(0)
        qk(ha, 1, 1)
        pv(ha, 0, 0)
        poll(1)
        qk(hb, 0, 0)
        pv(ha, 1, 1)
        store(ha).start()
        poll(2)
        qk(hb, 1, 1)
        pv(hb, 0, 0)
        poll(3)
        qk(hn, 0, 0)
        pv(hb, 1, 1)
        store(hb).start()
        return 0

    lax.fori_loop(0, 4, two_heads, 0)

    for g in range(4):
        l_sent(g)
    c_p().wait_send()
    for r in range(7):
        c_a0(r).wait_send()
        c_a2(r).wait_send()
        c_a3(r + 1).wait_send()
    for n in range(KV):
        c_cx(n, c).wait_send()
        store(n).wait()


def local(query_rows, token_keys, token_values, offsets, anchor_owner):
    exponents = np.arange(D // 2, dtype=np.float32) * np.float32(2.0 / D)
    inverse = (np.float64(ROPE_THETA) ** (-exponents.astype(np.float64))).astype(np.float32)
    inv = jnp.asarray(np.concatenate([inverse, inverse])[None, :])
    hbm = pl.BlockSpec(memory_space=pl.ANY)
    vmem = pl.BlockSpec(memory_space=pltpu.VMEM)
    smem = pl.BlockSpec(memory_space=pltpu.SMEM)
    dma = pltpu.SemaphoreType.DMA
    return pl.pallas_call(
        kernel,
        out_shape=jax.ShapeDtypeStruct(query_rows.shape, BF16),
        in_specs=[hbm, vmem, vmem, vmem, smem, smem],
        out_specs=hbm,
        scratch_shapes=[
            pltpu.VMEM((TOK, QUERY_HEADS * D), BF16),
            pltpu.VMEM((TOK, QUERY_HEADS * D), BF16),
            pltpu.VMEM((2, KV, 4, 2, TOK, D), BF16),
            pltpu.VMEM((2, KV, 8, TOK, D), BF16),
            pltpu.VMEM((2, KV, TOK, D), BF16),
            pltpu.VMEM((KV, TOK, D), BF16),
            pltpu.VMEM((KV, TOK, D), BF16),
            pltpu.VMEM((QUERY_HEADS * TOK, D), BF16),
            pltpu.VMEM((2, R, 2048), F32),
            pltpu.VMEM((2, R, D), F32),
            pltpu.VMEM((TOK, 256), F32),
            pltpu.VMEM((1024, D), BF16),
            pltpu.VMEM((TOK, D), F32),
            pltpu.VMEM((TOK, D), F32),
            dma, dma((8,)), dma((4,)), dma((4,)), dma((4, 4)), dma((4, 4)), dma((4, 4)), dma((4, 4)),
            dma((4,)), dma((4,)), dma((4,)), dma, dma, dma((8,)), dma((8,)), dma((8,)), dma((8,)),
            dma((8,)), dma((8,)), dma((8,)), dma((8,)),
        ],
        compiler_params=pltpu.CompilerParams(
            collective_id=0, has_side_effects=True, vmem_limit_bytes=60 * 2**20
        ),
        name="star_attention",
    )(query_rows, token_keys, token_values, inv, offsets, anchor_owner)


def solution(mesh):
    return jax.shard_map(
        local,
        mesh=mesh,
        in_specs=(
            P(("hst", "head"), None),
            P(("hst", "head"), None),
            P(("hst", "head"), None),
            P("hst"),
            P(),
        ),
        out_specs=P(("hst", "head"), None),
        check_vma=False,
    )
```

time: 415 us -> 63.7 us (0.15)
  waiting for transfers between devices: 261 us -> 0 us
  matrix products: 79.8 us -> 0 us
  Pallas kernels: 0 us -> 59.1 us
  local copies, waits for them, and re-layouts: 31.9 us -> 3.1 us
  other arithmetic: 21.9 us -> 0 us
  between operations: 16.5 us -> 1.3 us
    psum x1 -> x0, waiting for transfers between devices: 166 us -> none  [spread(): return lax.psum(jnp.where(mine, value, jnp.zeros_like(value)), axis)]
    all_gather x4 -> x0, waiting for transfers between devices: 92.7 us -> none  [the longest x1 53.8 us: local(): lax.all_gather(anchor_k, 'head', axis=0, tiled=True)]
    pallas_call x0 -> x1, Pallas kernels: none -> 59.1 us  [local(): pl.pallas_call(kernel, out_shape=jax.ShapeDtypeStruct(query_rows.shape, B...]
    sub x8 -> x0, matrix products: 51.2 us -> none  [attend(): weights = jnp.where(allowed[None], jnp.exp(scores - peak), jnp.float32(0.0))]
    dot_general x8 -> x0, matrix products: 28.6 us -> none  [attend(): jnp.einsum('grk,kd->grd', weights.astype(jnp.bfloat16), values_all, prefe...]
    dynamic_slice x48 -> x0, local copies, waits for them, and re-layouts: 22.5 us -> none  [local(): lax.map(per_kv_head, (jnp.transpose(spun_queries, (1, 0, 2, 3)), jnp.tran...]
    select_n x10 -> x0, other arithmetic: 13.7 us -> none  [the longest x8 12 us: attend(): jnp.where(column[None, :] < count, with_anchor, column[None, :] - count <...]
    unnamed x12 -> x1, local copies, waits for them, and re-layouts: 8.01 us -> 3.1 us
  transfers between devices with their start and end apart: 5 -> 0, of which waited for: 3 -> 0; matrix products, arithmetic and copies ran while one was open for 3% -> 0% of each run, Pallas kernels for 0% -> 0%
where the time goes in v1:
time: 63.7 us; the launch traced here: 63.5 us
  Pallas kernels  59.1 us (93%)
  local copies, waits for them, and re-layouts  3.1 us (5%)
  between operations  1.3 us (2%)
    pallas_call x1, Pallas kernels, local(): pl.pallas_call(kernel, out_shape=jax.ShapeDtypeStruct(query_rows.shape, B...  59.1 us
    unnamed x1, local copies, waits for them, and re-layouts  3.1 us

profile of v1, /device:TPU:27, one launch (start us, length us, event | category | flops | bytes accessed | tf_op | source)
XLA Modules:
  0.0 63.5 jit_solution(15870909495036788169)
XLA Ops:
  1.3 59.1 %star_attention.1 = bf16[128,8192]{1,0:T(8,128)(2,1)} custom-call(bf16[128,8192]{1,0:T(8,128)(2,1)} %q_ref.1, bf16[128,1024]{1,0:T(8,128)(2,1)} %k_ref.1, bf16[128,1024]{1,0:T(8,128)(2,1)} %v_ref.1, f32[1,128]{1,0:T(1,128)} %constant.2.clone.inv_ref, s32[1]{0:T(128)S(6)} %copy.8.off_ref, s32[1]{0:T(128)S(6)} %copy.9.own_ref), custom_call_target="tpu_custom_call" | custom-call | tf_op jit(solution)/shard_map/star_attention/pallas_call | solution.py:414
  60.4 3.1 %copy.10 = bf16[128,8192]{1,0:T(8,128)(2,1)} copy(bf16[128,8192]{1,0:T(8,128)(2,1)} %star_attention.1) | data formatting | bytes 4194304
